TPU v7x, 32 devices: a whole 2x2x4 slice. The times are simulated.
32 devices in a mesh: groups: 2 (over x), tiles: 16 (over z, y, core).
Axes of the slice: x: 2, y: 2, z: 4, core: 2. Of those that a mesh axis runs over, the one named last changes fastest.
Arguments:
- dipoles: bfloat16 [32, 2, 32, 384], P(('groups', 'tiles')), parts along dimension 0, may hold values from -6 to 6
- incident: bfloat16 [32, 2, 32, 384], P(('groups', 'tiles')), parts along dimension 0, may hold values from -6 to 6
- positions: float32 [32, 3, 128], P(('groups', 'tiles')), parts along dimension 0, may hold values from -44 to 44, as said below
- susceptibility: float32 [32, 128], P(('groups', 'tiles')), parts along dimension 0, may hold values from 0.05 to 0.5
- skeleton_sets: int32 [32, 128], P(('groups', 'tiles')), parts along dimension 0, may hold values from 0 to 767, as said below
- near_tiles: int32 [32, 2], P(('groups', 'tiles')), parts along dimension 0, may hold values from 0 to 7, as said below
- compress_fund: bfloat16 [32, 256, 384], P(('groups', 'tiles')), parts along dimension 0, may hold values from -0.21875 to 0.21875
- compress_harm: bfloat16 [32, 256, 384], P(('groups', 'tiles')), parts along dimension 0, may hold values from -0.21875 to 0.21875
Outputs:
- fundamental: float32 [32, 2, 32, 384], P(('groups', 'tiles')), parts along dimension 0
- adjoint_field: float32 [32, 2, 32, 384], P(('groups', 'tiles')), parts along dimension 0
There are 2 independent parts, one for each index of `groups`. A program takes and returns all parts, laid end to end along the dimension named above; each array names one. Nothing has to cross between parts.
Inputs may be any that keep to these rules, and one draw needn't show every extreme that they name: `skeleton_sets`: the 256 entries of tile t (rows 2t and 2t + 1 in order) are distinct. `near_tiles`: each row holds 2 distinct tiles, each differing from the row's own tile s // 2 by 1 or 2 in either direction, cyclically modulo 8. `positions`: distinct points lie at least 1 apart.
All inputs are finite; a program needn't handle non-finite values.
Results may differ from a plain program's by a relative error of at most 0.0051.
Values may be sent and summed in bfloat16 or wider, within the bound.
A program may use at most 128 MiB of HBM per device.

v0:
```python
import math

import jax
import jax.numpy as jnp
from jax import lax
from jax.experimental import pallas as pl
from jax.experimental.pallas import tpu as pltpu
from jax.sharding import PartitionSpec as P

POINTS = 256
SKELETONS = 256
ANGLES = 32
HALF = 128
ROWS = 2 * ANGLES
UNKNOWNS = 3 * HALF
CHUNK = 16

fund_wave = 0.5
harm_wave = 1.0

PI_HIGH = 3.140625
PI_LOW = math.pi - 3.140625
COS = (-0.4999993031990062, 0.04166394733655344, -0.0013855657175274386, 2.3189013831140122e-05)
SIN = (-0.16666656730445154, 0.008333010303754999, -0.00019806200404944314, 2.5992746473408684e-06)


def dot_nt(left, right):
    return lax.dot_general(
        left, right, (((1,), (1,)), ((), ())), preferred_element_type=jnp.float32
    )


def pair_terms(target, source, wave, sign):
    diff = [target[a] - source[a] for a in range(3)]
    squared = diff[0] * diff[0] + diff[1] * diff[1] + diff[2] * diff[2]
    present = squared > 0.0
    squared = jnp.where(present, squared, 1.0)
    inverse = lax.rsqrt(squared)
    phase = squared * inverse * wave
    turns = jnp.floor(phase * (1.0 / math.pi) + 0.5)
    rest = (phase - turns * PI_HIGH) - turns * PI_LOW
    half_turns = turns * 0.5
    odd = half_turns - jnp.floor(half_turns)
    amplitude = jnp.where(present, inverse * 0.5, 0.0) * (1.0 - 4.0 * odd)
    rest_sq = rest * rest
    cosine = 1.0 + rest_sq * (
        COS[0] + rest_sq * (COS[1] + rest_sq * (COS[2] + rest_sq * COS[3]))
    )
    sine = rest + rest * rest_sq * (
        SIN[0] + rest_sq * (SIN[1] + rest_sq * (SIN[2] + rest_sq * SIN[3]))
    )
    cosine = cosine * amplitude
    sine = sine * amplitude
    unit = [d * inverse for d in diff]
    z = inverse if wave == 1.0 else inverse * (1.0 / wave)
    z_sq = z * z
    one = 1.0 - z_sq
    three = 3.0 * z_sq - 1.0
    cos_z = cosine * z
    sin_z = sine * z
    same_real = cosine * one - sin_z
    same_imag = sine * one + cos_z
    along_real = cosine * three + 3.0 * sin_z
    along_imag = sine * three - 3.0 * cos_z
    if sign < 0:
        same_imag = -same_imag
        along_imag = -along_imag
    return unit, (same_real, same_imag), (along_real, along_imag)


def body(
    slabs,
    fields_ref,
    incident_ref,
    pos_ref,
    chi_ref,
    skel_ref,
    near_ref,
    vf_ref,
    vh_ref,
    fund_ref,
    adj_ref,
    target_ref,
    pos_all,
    skel_all,
    raw_first,
    raw_second,
    chg_first,
    chg_second,
    part_out,
    part_in,
    near_k,
    far_k,
    acc_ref,
    pos_send,
    pos_recv,
    skel_send,
    skel_recv,
    raw_send,
    raw_recv,
    chg_send,
    chg_recv,
    part_send,
    part_recv,
):
    tiles = slabs // 2
    raw_all = (raw_first, raw_second)
    chg_all = (chg_first, chg_second)
    group = lax.axis_index("groups")
    me = lax.axis_index("tiles")
    own_tile = lax.div(me, 2)
    my_half = lax.rem(me, 2)
    partner = own_tile * 2 + (1 - my_half)

    def peer(step):
        return lax.rem(me + step, slabs)

    def wrap_tile(t):
        return lax.rem(t + tiles, tiles)

    near_peers = [(partner, 4 + (1 - my_half), 4 + my_half)]
    for d in (-1, 1, -2, 2):
        for h in range(2):
            slab = wrap_tile(own_tile + d) * 2 + h
            near_peers.append((slab, (d + 2) * 2 + h, (2 - d) * 2 + my_half))

    barrier = pltpu.get_barrier_semaphore()

    def greet(step, carry):
        pl.semaphore_signal(
            barrier, inc=1, device_id=(group, peer(step)), device_id_type=pl.DeviceIdType.MESH
        )
        return carry

    lax.fori_loop(1, slabs, greet, 0)

    def copy(src, dst, send, recv, slab):
        return pltpu.make_async_remote_copy(
            src_ref=src,
            dst_ref=dst,
            send_sem=send,
            recv_sem=recv,
            device_id=(group, slab),
            device_id_type=pl.DeviceIdType.MESH,
        )

    def partial(phase, fields, v_ref):
        part_out[phase, 0] = dot_nt(fields, v_ref[0:HALF, :])
        part_out[phase, 1] = dot_nt(fields, v_ref[HALF:, :])

    def part_copy(phase):
        return copy(
            part_out.at[phase, 1 - my_half],
            part_in.at[phase],
            part_send.at[phase],
            part_recv.at[phase],
            partner,
        )

    own_slot = 4 + my_half

    def raw_copy(phase, number):
        slab, here, there = near_peers[number]
        return copy(
            raw_all[phase].at[own_slot],
            raw_all[phase].at[there],
            raw_send.at[phase, number],
            raw_recv.at[phase, there],
            slab,
        )

    def raw_arrival(phase, number):
        slab, here, there = near_peers[number]
        return copy(
            raw_all[phase].at[own_slot],
            raw_all[phase].at[here],
            raw_send.at[phase, number],
            raw_recv.at[phase, here],
            slab,
        )

    def pos_copy(number):
        slab, here, there = near_peers[number]
        return copy(
            pos_all.at[own_slot],
            pos_all.at[there],
            pos_send.at[number],
            pos_recv.at[there],
            slab,
        )

    def pos_arrival(number):
        slab, here, there = near_peers[number]
        return copy(
            pos_all.at[own_slot],
            pos_all.at[here],
            pos_send.at[number],
            pos_recv.at[here],
            slab,
        )

    def skel_copy(step, slot):
        return copy(
            skel_all.at[me], skel_all.at[slot], skel_send.at[step], skel_recv.at[slot], peer(step)
        )

    def chg_copy(phase, step, slot):
        return copy(
            chg_all[phase].at[me],
            chg_all[phase].at[slot],
            chg_send.at[phase, step],
            chg_recv.at[phase, slot],
            peer(step),
        )

    def each_peer(act):
        def go(step, carry):
            act(step)
            return carry

        lax.fori_loop(1, slabs, go, 0)

    def send_charges(phase):
        part_copy(phase).wait_recv()
        summed = part_out[phase, my_half] + part_in[phase]
        chg_all[phase][me] = summed.astype(jnp.bfloat16)
        each_peer(lambda step: chg_copy(phase, step, me).start())

    first, second = near_ref[0, 0], near_ref[0, 1]

    def near_slot(t):
        d = t - own_tile + 2
        d = jnp.where(d < 0, d + tiles, d)
        d = jnp.where(d >= tiles, d - tiles, d)
        return jnp.minimum(jnp.maximum(d, 0), 4)

    def near_place(place):
        return near_slot(
            jnp.where(place == 0, own_tile, jnp.where(place == 1, first, second))
        )

    low = jnp.minimum(own_tile, jnp.minimum(first, second))
    high = jnp.maximum(own_tile, jnp.maximum(first, second))
    middle = own_tile + first + second - low - high

    def far_tile(number):
        t = jnp.where(number >= low, number + 1, number)
        t = jnp.where(t >= middle, t + 1, t)
        return jnp.minimum(jnp.where(t >= high, t + 1, t), tiles - 1)

    def near_eval(place, half, wave, sign, own):
        block = pos_all[4 + half if own else near_place(place) * 2 + half]
        source = [block[a : a + 1, :] for a in range(3)]
        for chunk in range(HALF // CHUNK):
            rows = slice(chunk * CHUNK, (chunk + 1) * CHUNK)
            target = [target_ref[a, rows, :] for a in range(3)]
            unit, same, along = pair_terms(target, source, wave, sign)
            for part in range(2):
                scaled = [along[part] * unit[a] for a in range(3)]
                for a in range(3):
                    for b in range(a, 3):
                        value = scaled[a] * unit[b]
                        if a == b:
                            value = value + same[part]
                        value = value.astype(jnp.bfloat16)
                        for p, q in [(a, b), (b, a)][: 1 + (a != b)]:
                            start = part * UNKNOWNS + p * HALF + chunk * CHUNK
                            near_k[
                                place * 2 + half, start : start + CHUNK, q * HALF : (q + 1) * HALF
                            ] = value

    def far_eval(number, half, wave, sign):
        block = skel_all[far_tile(number) * 2 + half]
        source = [block[a : a + 1, :] for a in range(3)]
        which = [block[3 + a : 4 + a, :] for a in range(3)]
        for chunk in range(HALF // CHUNK):
            rows = slice(chunk * CHUNK, (chunk + 1) * CHUNK)
            target = [target_ref[a, rows, :] for a in range(3)]
            unit, same, along = pair_terms(target, source, wave, sign)
            projected = unit[0] * which[0] + unit[1] * which[1] + unit[2] * which[2]
            for part in range(2):
                scaled = along[part] * projected
                for a in range(3):
                    value = scaled * unit[a] + same[part] * which[a]
                    start = part * UNKNOWNS + a * HALF + chunk * CHUNK
                    far_k[number * 2 + half, start : start + CHUNK, :] = value.astype(jnp.bfloat16)

    def eval_near_from(start, stop, wave, sign):
        def go(index, carry):
            near_eval(lax.div(index, 2), lax.rem(index, 2), wave, sign, start == 0)
            return carry

        lax.fori_loop(2 * start, 2 * stop, go, 0)

    def eval_far(wave, sign):
        def go(index, carry):
            far_eval(lax.div(index, 2), lax.rem(index, 2), wave, sign)
            return carry

        lax.fori_loop(0, 2 * (tiles - 3), go, 0)

    def multiply_near(phase):
        def go(place, carry):
            slot = near_place(place) * 2
            acc_ref[...] += dot_nt(raw_all[phase][slot], near_k[place * 2]) + dot_nt(
                raw_all[phase][slot + 1], near_k[place * 2 + 1]
            )
            return carry

        lax.fori_loop(0, 3, go, 0)

    def multiply_far(phase):
        def go(number, carry):
            slot = far_tile(number) * 2
            charges = jnp.concatenate([chg_all[phase][slot], chg_all[phase][slot + 1]], axis=1)
            columns = jnp.concatenate([far_k[number * 2], far_k[number * 2 + 1]], axis=1)
            acc_ref[...] += dot_nt(charges, columns)
            return carry

        lax.fori_loop(0, tiles - 3, go, 0)

    def combined():
        real = acc_ref[:ANGLES, :UNKNOWNS] - acc_ref[ANGLES:, UNKNOWNS:]
        imag = acc_ref[:ANGLES, UNKNOWNS:] + acc_ref[ANGLES:, :UNKNOWNS]
        return real, imag

    raw_all[0][own_slot] = fields_ref[...]
    pos_all[own_slot, 0:3, :] = pos_ref[...]
    pos_all[own_slot, 3:8, :] = jnp.zeros((5, HALF), jnp.float32)
    partial(0, fields_ref[...], vf_ref)
    for a in range(3):
        target_ref[a] = jnp.broadcast_to(pos_ref[a : a + 1, :], (HALF, HALF)).T
    pl.semaphore_wait(barrier, slabs - 1)
    for number in range(9):
        pos_copy(number).start()
    part_copy(0).start()
    for number in range(9):
        raw_copy(0, number).start()
    acc_ref[...] = jnp.zeros_like(acc_ref)

    pos_arrival(0).wait_recv()
    skeleton = skel_ref[...]
    component = jnp.where(skeleton >= 2 * POINTS, 2, jnp.where(skeleton >= POINTS, 1, 0))
    point = skeleton - component * POINTS
    lines = lax.broadcasted_iota(jnp.int32, (HALF, HALF), 0)
    masks = [lines + HALF * h == point for h in range(2)]
    other = pos_all[4 + (1 - my_half)]
    packet = []
    for a in range(3):
        own_column = target_ref[a]
        other_column = jnp.broadcast_to(other[a : a + 1, :], (HALF, HALF)).T
        columns = [
            jnp.where(my_half == 0, own_column, other_column),
            jnp.where(my_half == 0, other_column, own_column),
        ]
        picked = jnp.where(masks[0], columns[0], jnp.where(masks[1], columns[1], 0.0))
        packet.append(jnp.sum(picked, axis=0, keepdims=True))
    for a in range(3):
        packet.append((component == a).astype(jnp.float32))
    packet.append(jnp.zeros((2, HALF), jnp.float32))
    skel_all[me] = jnp.concatenate(packet, axis=0)
    each_peer(lambda step: skel_copy(step, me).start())
    send_charges(0)

    eval_near_from(0, 1, fund_wave, 1.0)
    for number in range(1, 9):
        pos_arrival(number).wait_recv()
    eval_near_from(1, 3, fund_wave, 1.0)
    each_peer(lambda step: skel_copy(step, peer(step)).wait_recv())
    eval_far(fund_wave, 1.0)
    for number in range(9):
        raw_arrival(0, number).wait_recv()
    multiply_near(0)
    each_peer(lambda step: chg_copy(0, step, peer(step)).wait_recv())
    multiply_far(0)

    real, imag = combined()
    real = incident_ref[:ANGLES, :].astype(jnp.float32) + real
    imag = incident_ref[ANGLES:, :].astype(jnp.float32) + imag
    fund_ref[:ANGLES, :] = real
    fund_ref[ANGLES:, :] = imag
    weights = jnp.concatenate([chi_ref[...]] * 3, axis=1)
    source = jnp.concatenate(
        [weights * (real * real - imag * imag), weights * 2.0 * real * imag], axis=0
    ).astype(jnp.bfloat16)

    raw_all[1][own_slot] = source
    partial(1, source, vh_ref)
    part_copy(1).start()
    for number in range(9):
        raw_copy(1, number).start()
    acc_ref[...] = jnp.zeros_like(acc_ref)
    eval_near_from(0, 1, harm_wave, -1.0)
    send_charges(1)
    eval_near_from(1, 3, harm_wave, -1.0)
    eval_far(harm_wave, -1.0)
    for number in range(9):
        raw_arrival(1, number).wait_recv()
    multiply_near(1)
    each_peer(lambda step: chg_copy(1, step, peer(step)).wait_recv())
    multiply_far(1)
    real, imag = combined()
    adj_ref[:ANGLES, :] = real
    adj_ref[ANGLES:, :] = imag

    for number in range(9):
        pos_copy(number).wait_send()
    for phase in range(2):
        part_copy(phase).wait_send()
        for number in range(9):
            raw_copy(phase, number).wait_send()
        each_peer(lambda step: chg_copy(phase, step, me).wait_send())
    each_peer(lambda step: skel_copy(step, me).wait_send())


def solution(mesh):
    slabs = mesh.shape["tiles"]
    tiles = slabs // 2
    bf16, f32 = jnp.bfloat16, jnp.float32
    dma = pltpu.SemaphoreType.DMA
    vmem = pl.BlockSpec(memory_space=pltpu.VMEM)

    def on_device(dipoles, incident, positions, chi, skeletons, near, vf, vh):
        fields = dipoles.reshape(ROWS, UNKNOWNS)
        out = jax.ShapeDtypeStruct((ROWS, UNKNOWNS), f32)
        fund, adj = pl.pallas_call(
            lambda *refs: body(slabs, *refs),
            out_shape=(out, out),
            in_specs=[vmem] * 5 + [pl.BlockSpec(memory_space=pltpu.SMEM)] + [vmem] * 2,
            out_specs=(vmem, vmem),
            scratch_shapes=[
                pltpu.VMEM((3, HALF, HALF), f32),
                pltpu.VMEM((10, 8, HALF), f32),
                pltpu.VMEM((slabs, 8, HALF), f32),
                pltpu.VMEM((10, ROWS, UNKNOWNS), bf16),
                pltpu.VMEM((10, ROWS, UNKNOWNS), bf16),
                pltpu.VMEM((slabs, ROWS, HALF), bf16),
                pltpu.VMEM((slabs, ROWS, HALF), bf16),
                pltpu.VMEM((2, 2, ROWS, HALF), f32),
                pltpu.VMEM((2, ROWS, HALF), f32),
                pltpu.VMEM((6, 2 * UNKNOWNS, UNKNOWNS), bf16),
                pltpu.VMEM((2 * (tiles - 3), 2 * UNKNOWNS, HALF), bf16),
                pltpu.VMEM((ROWS, 2 * UNKNOWNS), f32),
                dma((9,)),
                dma((10,)),
                dma((slabs,)),
                dma((slabs,)),
                dma((2, 9)),
                dma((2, 10)),
                dma((2, slabs)),
                dma((2, slabs)),
                dma((2,)),
                dma((2,)),
            ],
            compiler_params=pltpu.CompilerParams(
                collective_id=0, has_side_effects=True, vmem_limit_bytes=50 * 2**20
            ),
            name="images",
        )(
            fields,
            incident.reshape(ROWS, UNKNOWNS),
            positions[0],
            chi,
            skeletons,
            near,
            vf[0],
            vh[0],
        )
        shape = (1, 2, ANGLES, UNKNOWNS)
        return fund.reshape(shape), adj.reshape(shape)

    row = ("groups", "tiles")
    in_specs = (
        P(row, None, None, None),
        P(row, None, None, None),
        P(row, None, None),
        P(row, None),
        P(row, None),
        P(row, None),
        P(row, None, None),
        P(row, None, None),
    )
    out_specs = (P(row, None, None, None), P(row, None, None, None))
    return jax.shard_map(
        on_device, mesh=mesh, in_specs=in_specs, out_specs=out_specs, check_vma=False
    )
```

profile of v0, /device:TPU:0, one launch (start us, length us, event | category | flops | bytes accessed | tf_op | source)
XLA Modules:
  0.0 47.0 jit_solution(2434994425617491254)
XLA Ops:
  0.6 0.0 copy-start.7
  0.6 0.7 %copy-done.7 = f32[1,3,128]{2,0,1:T(1,128)S(1)} copy-done((f32[1,3,128]{2,0,1:T(1,128)S(1)}, f32[1,3,128]{2,0,1:T(1,128)}, u32[]{:S(2)}) %copy-start.7) | copy-done | bytes 1560
  1.3 0.0 copy-start.4
  1.3 0.0 copy-start.5
  1.3 0.0 copy-start.6
  1.3 0.6 %copy-done.4 = f32[1,128]{1,0:T(1,128)S(1)} copy-done((f32[1,128]{1,0:T(1,128)S(1)}, f32[1,128]{1,0:T(1,128)}, u32[]{:S(2)}) %copy-start.4) | copy-done | bytes 536
  2.0 0.0 copy-done.5
  2.0 0.0 copy-done.6
  2.0 0.0 copy-start
  2.0 0.9 %copy-done = bf16[1,256,384]{2,1,0:T(8,128)(2,1)S(1)} copy-done((bf16[1,256,384]{2,1,0:T(8,128)(2,1)S(1)}, bf16[1,256,384]{2,1,0:T(8,128)(2,1)}, u32[]{:S(2)}) %copy-start) | copy-done | bytes 196632
  2.9 0.0 copy-start.1
  2.9 0.9 %copy-done.1 = bf16[1,256,384]{2,1,0:T(8,128)(2,1)S(1)} copy-done((bf16[1,256,384]{2,1,0:T(8,128)(2,1)S(1)}, bf16[1,256,384]{2,1,0:T(8,128)(2,1)}, u32[]{:S(2)}) %copy-start.1) | copy-done | bytes 196632
  3.9 0.0 copy-start.2
  3.9 0.8 %copy-done.2 = bf16[1,2,32,384]{3,2,1,0:T(8,128)(2,1)S(1)} copy-done((bf16[1,2,32,384]{3,2,1,0:T(8,128)(2,1)S(1)}, bf16[1,2,32,384]{3,2,1,0:T(8,128)(2,1)}, u32[]{:S(2)}) %copy-start.2) | copy-done | bytes 49176
  4.7 0.0 copy-start.3
  4.7 0.8 %copy-done.3 = bf16[1,2,32,384]{3,2,1,0:T(8,128)(2,1)S(1)} copy-done((bf16[1,2,32,384]{3,2,1,0:T(8,128)(2,1)S(1)}, bf16[1,2,32,384]{3,2,1,0:T(8,128)(2,1)}, u32[]{:S(2)}) %copy-start.3) | copy-done | bytes 49176
  5.5 40.2 %images.1 = (f32[64,384]{1,0:T(8,128)S(1)}, f32[64,384]{1,0:T(8,128)S(1)}) custom-call(bf16[64,384]{1,0:T(8,128)(2,1)S(1)} %bitcast.13, bf16[64,384]{1,0:T(8,128)(2,1)S(1)} %bitcast.14, f32[3,128]{1,0:T(4,128)S(1)} %bitcast.15, f32[1,128]{1,0:T(1,128)S(1)} %copy-done.4, s32[1,128]{1,0:T(1,128)S(1)} %copy-done.5, s32[1,2]{1,0:T(1,128)S(1)} %copy-done.6, ...), custom_call_target="tpu_custom_call" | custom-call | tf_op jit(solution)/shard_map/images/pallas_call | solution.py:426
  45.7 0.6 %copy.15 = f32[1,2,32,384]{3,2,1,0:T(8,128)} copy(f32[1,2,32,384]{3,2,1,0:T(8,128)S(1)} %bitcast.12) | data formatting | bytes 196608
  46.3 0.6 %copy.16 = f32[1,2,32,384]{3,2,1,0:T(8,128)} copy(f32[1,2,32,384]{3,2,1,0:T(8,128)S(1)} %bitcast.11) | data formatting | bytes 196608
  (1 shorter events, 0.0 us)
Async XLA Ops:
  0.6 0.7 %copy-start.7 = (f32[1,3,128]{2,0,1:T(1,128)S(1)}, f32[1,3,128]{2,0,1:T(1,128)}, u32[]{:S(2)}) copy-start(f32[1,3,128]{2,0,1:T(1,128)} %param.10) | copy-start | bytes 4612
  1.3 0.7 %copy-start.4 = (f32[1,128]{1,0:T(1,128)S(1)}, f32[1,128]{1,0:T(1,128)}, u32[]{:S(2)}) copy-start(f32[1,128]{1,0:T(1,128)} %refs_3_.1) | copy-start | bytes 1540
  1.3 0.7 %copy-start.5 = (s32[1,128]{1,0:T(1,128)S(1)}, s32[1,128]{1,0:T(1,128)}, u32[]{:S(2)}) copy-start(s32[1,128]{1,0:T(1,128)} %refs_4_.1) | copy-start | bytes 1540
  1.3 0.7 %copy-start.6 = (s32[1,2]{1,0:T(1,128)S(1)}, s32[1,2]{1,0:T(1,128)}, u32[]{:S(2)}) copy-start(s32[1,2]{1,0:T(1,128)} %refs_5_.1) | copy-start | bytes 28
  2.0 0.9 %copy-start = (bf16[1,256,384]{2,1,0:T(8,128)(2,1)S(1)}, bf16[1,256,384]{2,1,0:T(8,128)(2,1)}, u32[]{:S(2)}) copy-start(bf16[1,256,384]{2,1,0:T(8,128)(2,1)} %param.14) | copy-start | bytes 589828
  2.9 0.9 %copy-start.1 = (bf16[1,256,384]{2,1,0:T(8,128)(2,1)S(1)}, bf16[1,256,384]{2,1,0:T(8,128)(2,1)}, u32[]{:S(2)}) copy-start(bf16[1,256,384]{2,1,0:T(8,128)(2,1)} %param.15) | copy-start | bytes 589828
  3.9 0.8 %copy-start.2 = (bf16[1,2,32,384]{3,2,1,0:T(8,128)(2,1)S(1)}, bf16[1,2,32,384]{3,2,1,0:T(8,128)(2,1)}, u32[]{:S(2)}) copy-start(bf16[1,2,32,384]{3,2,1,0:T(8,128)(2,1)} %param.8) | copy-start | bytes 147460
  4.7 0.8 %copy-start.3 = (bf16[1,2,32,384]{3,2,1,0:T(8,128)(2,1)S(1)}, bf16[1,2,32,384]{3,2,1,0:T(8,128)(2,1)}, u32[]{:S(2)}) copy-start(bf16[1,2,32,384]{3,2,1,0:T(8,128)(2,1)} %param.9) | copy-start | bytes 147460
where the time goes:
time: 47.3 us; the launch traced here: 47 us
  Pallas kernels  40.2 us (85%)
  local copies, waits for them, and re-layouts  6.09 us (13%)
  between operations  0.66 us (1%)
    pallas_call x1, Pallas kernels, on_device(): pl.pallas_call(lambda *refs: body(slabs, *refs), out_shape=(out, out), in...  40.2 us
    unnamed x19, local copies, waits for them, and re-layouts  6.09 us

commit v1 on v0

--- a/solution.py
+++ b/solution.py
@@ -70,16 +70,21 @@
 
 def body(
     slabs,
-    fields_ref,
+    fields_in,
+    incident_in,
+    pos_in,
+    chi_in,
+    skel_in,
+    near_ref,
+    vf_in,
+    vh_in,
+    fund_ref,
+    adj_ref,
     incident_ref,
-    pos_ref,
     chi_ref,
     skel_ref,
-    near_ref,
     vf_ref,
     vh_ref,
-    fund_ref,
-    adj_ref,
     target_ref,
     pos_all,
     skel_all,
@@ -102,6 +107,7 @@
     chg_recv,
     part_send,
     part_recv,
+    load_sem,
 ):
     tiles = slabs // 2
     raw_all = (raw_first, raw_second)
@@ -113,16 +119,16 @@
     partner = own_tile * 2 + (1 - my_half)
 
     def peer(step):
-        return lax.rem(me + step, slabs)
+        return lax.rem(me + 2 * step, slabs)
 
     def wrap_tile(t):
         return lax.rem(t + tiles, tiles)
 
-    near_peers = [(partner, 4 + (1 - my_half), 4 + my_half)]
-    for d in (-1, 1, -2, 2):
-        for h in range(2):
-            slab = wrap_tile(own_tile + d) * 2 + h
-            near_peers.append((slab, (d + 2) * 2 + h, (2 - d) * 2 + my_half))
+    near_peers = [(d, wrap_tile(own_tile + d) * 2 + my_half) for d in (-1, 1, -2, 2)]
+    own_slot = 4 + my_half
+
+    def slot_of(d, half):
+        return (d + 2) * 2 + half
 
     barrier = pltpu.get_barrier_semaphore()
 
@@ -132,7 +138,10 @@
         )
         return carry
 
-    lax.fori_loop(1, slabs, greet, 0)
+    pl.semaphore_signal(
+        barrier, inc=1, device_id=(group, partner), device_id_type=pl.DeviceIdType.MESH
+    )
+    lax.fori_loop(1, tiles, greet, 0)
 
     def copy(src, dst, send, recv, slab):
         return pltpu.make_async_remote_copy(
@@ -157,74 +166,82 @@
             partner,
         )
 
-    own_slot = 4 + my_half
-
-    def raw_copy(phase, number):
-        slab, here, there = near_peers[number]
-        return copy(
-            raw_all[phase].at[own_slot],
-            raw_all[phase].at[there],
-            raw_send.at[phase, number],
-            raw_recv.at[phase, there],
-            slab,
-        )
-
-    def raw_arrival(phase, number):
-        slab, here, there = near_peers[number]
-        return copy(
-            raw_all[phase].at[own_slot],
-            raw_all[phase].at[here],
-            raw_send.at[phase, number],
-            raw_recv.at[phase, here],
-            slab,
-        )
-
-    def pos_copy(number):
-        slab, here, there = near_peers[number]
-        return copy(
-            pos_all.at[own_slot],
-            pos_all.at[there],
-            pos_send.at[number],
-            pos_recv.at[there],
-            slab,
-        )
-
-    def pos_arrival(number):
-        slab, here, there = near_peers[number]
-        return copy(
-            pos_all.at[own_slot],
-            pos_all.at[here],
-            pos_send.at[number],
-            pos_recv.at[here],
-            slab,
-        )
-
-    def skel_copy(step, slot):
-        return copy(
-            skel_all.at[me], skel_all.at[slot], skel_send.at[step], skel_recv.at[slot], peer(step)
-        )
-
-    def chg_copy(phase, step, slot):
-        return copy(
-            chg_all[phase].at[me],
-            chg_all[phase].at[slot],
-            chg_send.at[phase, step],
-            chg_recv.at[phase, slot],
-            peer(step),
-        )
-
-    def each_peer(act):
+    def near_sends(buffer, send, recv):
+        copy(buffer.at[own_slot], buffer.at[own_slot], send.at[0], recv.at[own_slot], partner).start()
+        for number, (d, slab) in enumerate(near_peers):
+            slot = slot_of(-d, my_half)
+            copy(buffer.at[own_slot], buffer.at[slot], send.at[1 + number], recv.at[slot], slab).start()
+
+    def near_wait(buffer, send, recv, slot):
+        copy(buffer.at[own_slot], buffer.at[slot], send.at[0], recv.at[slot], partner).wait_recv()
+
+    def near_forward(buffer, send, recv):
+        for number, (d, slab) in enumerate(near_peers):
+            slot = slot_of(d, my_half)
+            near_wait(buffer, send, recv, slot)
+            copy(buffer.at[slot], buffer.at[slot], send.at[5 + number], recv.at[slot], partner).start()
+
+    def near_arrive(buffer, send, recv, with_partner):
+        if with_partner:
+            near_wait(buffer, send, recv, 5 - my_half)
+        for d, slab in near_peers:
+            near_wait(buffer, send, recv, slot_of(d, 1 - my_half))
+
+    def near_sent(buffer, send, recv):
+        for number in range(9):
+            copy(
+                buffer.at[own_slot], buffer.at[own_slot], send.at[number], recv.at[own_slot], partner
+            ).wait_send()
+
+    def loop(act):
         def go(step, carry):
             act(step)
             return carry
 
-        lax.fori_loop(1, slabs, go, 0)
+        lax.fori_loop(1, tiles, go, 0)
+
+    def far_sends(buffer, send, recv):
+        copy(buffer.at[me], buffer.at[me], send.at[0], recv.at[me], partner).start()
+        loop(
+            lambda step: copy(
+                buffer.at[me], buffer.at[me], send.at[step], recv.at[me], peer(step)
+            ).start()
+        )
+
+    def far_wait(buffer, send, recv, slab):
+        copy(buffer.at[me], buffer.at[slab], send.at[0], recv.at[slab], partner).wait_recv()
+
+    def far_forward(buffer, send, recv):
+        def act(step):
+            slab = peer(step)
+            far_wait(buffer, send, recv, slab)
+            copy(
+                buffer.at[slab], buffer.at[slab], send.at[tiles - 1 + step], recv.at[slab], partner
+            ).start()
+
+        loop(act)
+
+    def far_arrive(buffer, send, recv):
+        far_wait(buffer, send, recv, partner)
+        loop(lambda step: far_wait(buffer, send, recv, lax.rem(partner + 2 * step, slabs)))
+
+    def far_sent(buffer, send, recv):
+        def go(number, carry):
+            copy(buffer.at[me], buffer.at[me], send.at[number], recv.at[me], partner).wait_send()
+            return carry
+
+        lax.fori_loop(0, slabs - 1, go, 0)
+
+    pos_set = (pos_all, pos_send, pos_recv)
+    skel_set = (skel_all, skel_send, skel_recv)
+    raw_set = [(raw_all[p], raw_send.at[p], raw_recv.at[p]) for p in range(2)]
+    chg_set = [(chg_all[p], chg_send.at[p], chg_recv.at[p]) for p in range(2)]
 
     def send_charges(phase):
         part_copy(phase).wait_recv()
         summed = part_out[phase, my_half] + part_in[phase]
         chg_all[phase][me] = summed.astype(jnp.bfloat16)
-        each_peer(lambda step: chg_copy(phase, step, me).start())
+        far_sends(*chg_set[phase])
 
     first, second = near_ref[0, 0], near_ref[0, 1]
 
@@ -292,12 +309,12 @@
 
         lax.fori_loop(2 * start, 2 * stop, go, 0)
 
-    def eval_far(wave, sign):
+    def eval_far(start, stop, wave, sign):
         def go(index, carry):
             far_eval(lax.div(index, 2), lax.rem(index, 2), wave, sign)
             return carry
 
-        lax.fori_loop(0, 2 * (tiles - 3), go, 0)
+        lax.fori_loop(2 * start, 2 * stop, go, 0)
 
     def multiply_near(phase):
         def go(place, carry):
@@ -324,21 +341,36 @@
         imag = acc_ref[:ANGLES, UNKNOWNS:] + acc_ref[ANGLES:, :UNKNOWNS]
         return real, imag
 
-    raw_all[0][own_slot] = fields_ref[...]
-    pos_all[own_slot, 0:3, :] = pos_ref[...]
-    pos_all[own_slot, 3:8, :] = jnp.zeros((5, HALF), jnp.float32)
-    partial(0, fields_ref[...], vf_ref)
+    loads = [
+        pltpu.make_async_copy(src, dst, load_sem.at[number])
+        for number, (src, dst) in enumerate(
+            [
+                (pos_in, pos_all.at[own_slot]),
+                (fields_in, raw_all[0].at[own_slot]),
+                (vf_in, vf_ref),
+                (skel_in, skel_ref),
+                (chi_in, chi_ref),
+                (incident_in, incident_ref),
+                (vh_in, vh_ref),
+            ]
+        )
+    ]
+    for load in loads:
+        load.start()
+    acc_ref[...] = jnp.zeros_like(acc_ref)
+    loads[0].wait()
     for a in range(3):
-        target_ref[a] = jnp.broadcast_to(pos_ref[a : a + 1, :], (HALF, HALF)).T
-    pl.semaphore_wait(barrier, slabs - 1)
-    for number in range(9):
-        pos_copy(number).start()
+        target_ref[a] = jnp.broadcast_to(pos_all[own_slot, a : a + 1, :], (HALF, HALF)).T
+    loads[1].wait()
+    loads[2].wait()
+    partial(0, raw_all[0][own_slot], vf_ref)
+    pl.semaphore_wait(barrier, tiles)
+    near_sends(*pos_set)
     part_copy(0).start()
-    for number in range(9):
-        raw_copy(0, number).start()
-    acc_ref[...] = jnp.zeros_like(acc_ref)
-
-    pos_arrival(0).wait_recv()
+    near_sends(*raw_set[0])
+    loads[3].wait()
+
+    near_wait(*pos_set, 5 - my_half)
     skeleton = skel_ref[...]
     component = jnp.where(skeleton >= 2 * POINTS, 2, jnp.where(skeleton >= POINTS, 1, 0))
     point = skeleton - component * POINTS
@@ -359,21 +391,28 @@
         packet.append((component == a).astype(jnp.float32))
     packet.append(jnp.zeros((2, HALF), jnp.float32))
     skel_all[me] = jnp.concatenate(packet, axis=0)
-    each_peer(lambda step: skel_copy(step, me).start())
+    far_sends(*skel_set)
     send_charges(0)
 
+    near_forward(*pos_set)
     eval_near_from(0, 1, fund_wave, 1.0)
-    for number in range(1, 9):
-        pos_arrival(number).wait_recv()
+    far_forward(*skel_set)
+    near_arrive(*pos_set, False)
     eval_near_from(1, 3, fund_wave, 1.0)
-    each_peer(lambda step: skel_copy(step, peer(step)).wait_recv())
-    eval_far(fund_wave, 1.0)
-    for number in range(9):
-        raw_arrival(0, number).wait_recv()
+    near_forward(*raw_set[0])
+    far_arrive(*skel_set)
+    split = (tiles - 3) // 2
+    eval_far(0, split, fund_wave, 1.0)
+    far_forward(*chg_set[0])
+    eval_far(split, tiles - 3, fund_wave, 1.0)
+    near_arrive(*raw_set[0], True)
     multiply_near(0)
-    each_peer(lambda step: chg_copy(0, step, peer(step)).wait_recv())
+    far_arrive(*chg_set[0])
     multiply_far(0)
 
+    loads[4].wait()
+    loads[5].wait()
+    loads[6].wait()
     real, imag = combined()
     real = incident_ref[:ANGLES, :].astype(jnp.float32) + real
     imag = incident_ref[ANGLES:, :].astype(jnp.float32) + imag
@@ -387,30 +426,29 @@
     raw_all[1][own_slot] = source
     partial(1, source, vh_ref)
     part_copy(1).start()
-    for number in range(9):
-        raw_copy(1, number).start()
+    near_sends(*raw_set[1])
     acc_ref[...] = jnp.zeros_like(acc_ref)
     eval_near_from(0, 1, harm_wave, -1.0)
     send_charges(1)
     eval_near_from(1, 3, harm_wave, -1.0)
-    eval_far(harm_wave, -1.0)
-    for number in range(9):
-        raw_arrival(1, number).wait_recv()
+    near_forward(*raw_set[1])
+    eval_far(0, split, harm_wave, -1.0)
+    far_forward(*chg_set[1])
+    eval_far(split, tiles - 3, harm_wave, -1.0)
+    near_arrive(*raw_set[1], True)
     multiply_near(1)
-    each_peer(lambda step: chg_copy(1, step, peer(step)).wait_recv())
+    far_arrive(*chg_set[1])
     multiply_far(1)
     real, imag = combined()
     adj_ref[:ANGLES, :] = real
     adj_ref[ANGLES:, :] = imag
 
-    for number in range(9):
-        pos_copy(number).wait_send()
+    near_sent(*pos_set)
+    far_sent(*skel_set)
     for phase in range(2):
         part_copy(phase).wait_send()
-        for number in range(9):
-            raw_copy(phase, number).wait_send()
-        each_peer(lambda step: chg_copy(phase, step, me).wait_send())
-    each_peer(lambda step: skel_copy(step, me).wait_send())
+        near_sent(*raw_set[phase])
+        far_sent(*chg_set[phase])
 
 
 def solution(mesh):
@@ -418,6 +456,7 @@
     tiles = slabs // 2
     bf16, f32 = jnp.bfloat16, jnp.float32
     dma = pltpu.SemaphoreType.DMA
+    hbm = pl.BlockSpec(memory_space=pltpu.HBM)
     vmem = pl.BlockSpec(memory_space=pltpu.VMEM)
 
     def on_device(dipoles, incident, positions, chi, skeletons, near, vf, vh):
@@ -426,11 +465,16 @@
         fund, adj = pl.pallas_call(
             lambda *refs: body(slabs, *refs),
             out_shape=(out, out),
-            in_specs=[vmem] * 5 + [pl.BlockSpec(memory_space=pltpu.SMEM)] + [vmem] * 2,
+            in_specs=[hbm] * 5 + [pl.BlockSpec(memory_space=pltpu.SMEM)] + [hbm] * 2,
             out_specs=(vmem, vmem),
             scratch_shapes=[
+                pltpu.VMEM((ROWS, UNKNOWNS), bf16),
+                pltpu.VMEM((1, HALF), f32),
+                pltpu.VMEM((1, HALF), jnp.int32),
+                pltpu.VMEM((SKELETONS, UNKNOWNS), bf16),
+                pltpu.VMEM((SKELETONS, UNKNOWNS), bf16),
                 pltpu.VMEM((3, HALF, HALF), f32),
-                pltpu.VMEM((10, 8, HALF), f32),
+                pltpu.VMEM((10, 3, HALF), f32),
                 pltpu.VMEM((slabs, 8, HALF), f32),
                 pltpu.VMEM((10, ROWS, UNKNOWNS), bf16),
                 pltpu.VMEM((10, ROWS, UNKNOWNS), bf16),
@@ -451,6 +495,7 @@
                 dma((2, slabs)),
                 dma((2,)),
                 dma((2,)),
+                dma((7,)),
             ],
             compiler_params=pltpu.CompilerParams(
                 collective_id=0, has_side_effects=True, vmem_limit_bytes=50 * 2**20

time: 47.3 us -> 41.2 us (0.87)
  Pallas kernels: 40.2 us -> 34.2 us
    pallas_call x1, Pallas kernels: 40.2 us -> 34.2 us  [on_device(): pl.pallas_call(lambda *refs: body(slabs, *refs), out_shape=(out, out), in...]
where the time goes in v1:
time: 41.2 us; the launch traced here: 40.9 us
  Pallas kernels  34.2 us (83%)
  local copies, waits for them, and re-layouts  6.09 us (15%)
  between operations  0.66 us (2%)
    pallas_call x1, Pallas kernels, on_device(): pl.pallas_call(lambda *refs: body(slabs, *refs), out_shape=(out, out), in...  34.2 us
    unnamed x19, local copies, waits for them, and re-layouts  6.09 us

profile of v1, /device:TPU:0, one launch (start us, length us, event | category | flops | bytes accessed | tf_op | source)
XLA Modules:
  0.0 40.9 jit_solution(719128512392521705)
XLA Ops:
  0.6 0.0 copy-start.7
  0.6 0.7 %copy-done.7 = f32[1,3,128]{2,0,1:T(1,128)S(1)} copy-done((f32[1,3,128]{2,0,1:T(1,128)S(1)}, f32[1,3,128]{2,0,1:T(1,128)}, u32[]{:S(2)}) %copy-start.7) | copy-done | bytes 1560
  1.3 0.0 copy-start.4
  1.3 0.0 copy-start.5
  1.3 0.0 copy-start.6
  1.3 0.6 %copy-done.4 = f32[1,128]{1,0:T(1,128)S(1)} copy-done((f32[1,128]{1,0:T(1,128)S(1)}, f32[1,128]{1,0:T(1,128)}, u32[]{:S(2)}) %copy-start.4) | copy-done | bytes 536
  2.0 0.0 copy-done.5
  2.0 0.0 copy-done.6
  2.0 0.0 copy-start
  2.0 0.9 %copy-done = bf16[1,256,384]{2,1,0:T(8,128)(2,1)S(1)} copy-done((bf16[1,256,384]{2,1,0:T(8,128)(2,1)S(1)}, bf16[1,256,384]{2,1,0:T(8,128)(2,1)}, u32[]{:S(2)}) %copy-start) | copy-done | bytes 196632
  2.9 0.0 copy-start.1
  2.9 0.9 %copy-done.1 = bf16[1,256,384]{2,1,0:T(8,128)(2,1)S(1)} copy-done((bf16[1,256,384]{2,1,0:T(8,128)(2,1)S(1)}, bf16[1,256,384]{2,1,0:T(8,128)(2,1)}, u32[]{:S(2)}) %copy-start.1) | copy-done | bytes 196632
  3.9 0.0 copy-start.2
  3.9 0.8 %copy-done.2 = bf16[1,2,32,384]{3,2,1,0:T(8,128)(2,1)S(1)} copy-done((bf16[1,2,32,384]{3,2,1,0:T(8,128)(2,1)S(1)}, bf16[1,2,32,384]{3,2,1,0:T(8,128)(2,1)}, u32[]{:S(2)}) %copy-start.2) | copy-done | bytes 49176
  4.7 0.0 copy-start.3
  4.7 0.8 %copy-done.3 = bf16[1,2,32,384]{3,2,1,0:T(8,128)(2,1)S(1)} copy-done((bf16[1,2,32,384]{3,2,1,0:T(8,128)(2,1)S(1)}, bf16[1,2,32,384]{3,2,1,0:T(8,128)(2,1)}, u32[]{:S(2)}) %copy-start.3) | copy-done | bytes 49176
  5.5 34.2 %images.1 = (f32[64,384]{1,0:T(8,128)S(1)}, f32[64,384]{1,0:T(8,128)S(1)}) custom-call(bf16[64,384]{1,0:T(8,128)(2,1)S(1)} %bitcast.13, bf16[64,384]{1,0:T(8,128)(2,1)S(1)} %bitcast.14, f32[3,128]{1,0:T(4,128)S(1)} %bitcast.15, f32[1,128]{1,0:T(1,128)S(1)} %copy-done.4, s32[1,128]{1,0:T(1,128)S(1)} %copy-done.5, s32[1,2]{1,0:T(1,128)S(1)} %copy-done.6, ...), custom_call_target="tpu_custom_call" | custom-call | tf_op jit(solution)/shard_map/images/pallas_call | solution.py:465
  39.7 0.6 %copy.15 = f32[1,2,32,384]{3,2,1,0:T(8,128)} copy(f32[1,2,32,384]{3,2,1,0:T(8,128)S(1)} %bitcast.12) | data formatting | bytes 196608
  40.3 0.6 %copy.16 = f32[1,2,32,384]{3,2,1,0:T(8,128)} copy(f32[1,2,32,384]{3,2,1,0:T(8,128)S(1)} %bitcast.11) | data formatting | bytes 196608
  (1 shorter events, 0.0 us)
Async XLA Ops:
  0.6 0.7 %copy-start.7 = (f32[1,3,128]{2,0,1:T(1,128)S(1)}, f32[1,3,128]{2,0,1:T(1,128)}, u32[]{:S(2)}) copy-start(f32[1,3,128]{2,0,1:T(1,128)} %param.10) | copy-start | bytes 4612
  1.3 0.7 %copy-start.4 = (f32[1,128]{1,0:T(1,128)S(1)}, f32[1,128]{1,0:T(1,128)}, u32[]{:S(2)}) copy-start(f32[1,128]{1,0:T(1,128)} %refs_3_.1) | copy-start | bytes 1540
  1.3 0.7 %copy-start.5 = (s32[1,128]{1,0:T(1,128)S(1)}, s32[1,128]{1,0:T(1,128)}, u32[]{:S(2)}) copy-start(s32[1,128]{1,0:T(1,128)} %refs_4_.1) | copy-start | bytes 1540
  1.3 0.7 %copy-start.6 = (s32[1,2]{1,0:T(1,128)S(1)}, s32[1,2]{1,0:T(1,128)}, u32[]{:S(2)}) copy-start(s32[1,2]{1,0:T(1,128)} %refs_5_.1) | copy-start | bytes 28
  2.0 0.9 %copy-start = (bf16[1,256,384]{2,1,0:T(8,128)(2,1)S(1)}, bf16[1,256,384]{2,1,0:T(8,128)(2,1)}, u32[]{:S(2)}) copy-start(bf16[1,256,384]{2,1,0:T(8,128)(2,1)} %param.14) | copy-start | bytes 589828
  2.9 0.9 %copy-start.1 = (bf16[1,256,384]{2,1,0:T(8,128)(2,1)S(1)}, bf16[1,256,384]{2,1,0:T(8,128)(2,1)}, u32[]{:S(2)}) copy-start(bf16[1,256,384]{2,1,0:T(8,128)(2,1)} %param.15) | copy-start | bytes 589828
  3.9 0.8 %copy-start.2 = (bf16[1,2,32,384]{3,2,1,0:T(8,128)(2,1)S(1)}, bf16[1,2,32,384]{3,2,1,0:T(8,128)(2,1)}, u32[]{:S(2)}) copy-start(bf16[1,2,32,384]{3,2,1,0:T(8,128)(2,1)} %param.8) | copy-start | bytes 147460
  4.7 0.8 %copy-start.3 = (bf16[1,2,32,384]{3,2,1,0:T(8,128)(2,1)S(1)}, bf16[1,2,32,384]{3,2,1,0:T(8,128)(2,1)}, u32[]{:S(2)}) copy-start(bf16[1,2,32,384]{3,2,1,0:T(8,128)(2,1)} %param.9) | copy-start | bytes 147460

commit v2 on v1

--- a/solution.py
+++ b/solution.py
@@ -14,6 +14,7 @@
 ROWS = 2 * ANGLES
 UNKNOWNS = 3 * HALF
 CHUNK = 16
+VMEM = 64 * 2**20 - 64 * 1024
 
 fund_wave = 0.5
 harm_wave = 1.0
@@ -154,8 +155,11 @@
         )
 
     def partial(phase, fields, v_ref):
-        part_out[phase, 0] = dot_nt(fields, v_ref[0:HALF, :])
-        part_out[phase, 1] = dot_nt(fields, v_ref[HALF:, :])
+        half = 1 - my_half
+        part_out[phase, half] = dot_nt(fields, v_ref[pl.ds(pl.multiple_of(half * HALF, HALF), HALF), :])
+        part_copy(phase).start()
+        half = my_half
+        part_out[phase, half] = dot_nt(fields, v_ref[pl.ds(pl.multiple_of(half * HALF, HALF), HALF), :])
 
     def part_copy(phase):
         return copy(
@@ -167,10 +171,12 @@
         )
 
     def near_sends(buffer, send, recv):
-        copy(buffer.at[own_slot], buffer.at[own_slot], send.at[0], recv.at[own_slot], partner).start()
         for number, (d, slab) in enumerate(near_peers):
             slot = slot_of(-d, my_half)
             copy(buffer.at[own_slot], buffer.at[slot], send.at[1 + number], recv.at[slot], slab).start()
+
+    def partner_send(buffer, send, recv):
+        copy(buffer.at[own_slot], buffer.at[own_slot], send.at[0], recv.at[own_slot], partner).start()
 
     def near_wait(buffer, send, recv, slot):
         copy(buffer.at[own_slot], buffer.at[slot], send.at[0], recv.at[slot], partner).wait_recv()
@@ -181,9 +187,7 @@
             near_wait(buffer, send, recv, slot)
             copy(buffer.at[slot], buffer.at[slot], send.at[5 + number], recv.at[slot], partner).start()
 
-    def near_arrive(buffer, send, recv, with_partner):
-        if with_partner:
-            near_wait(buffer, send, recv, 5 - my_half)
+    def near_arrive(buffer, send, recv):
         for d, slab in near_peers:
             near_wait(buffer, send, recv, slot_of(d, 1 - my_half))
 
@@ -265,9 +269,9 @@
         t = jnp.where(t >= middle, t + 1, t)
         return jnp.minimum(jnp.where(t >= high, t + 1, t), tiles - 1)
 
-    def near_eval(place, half, wave, sign, own):
-        block = pos_all[4 + half if own else near_place(place) * 2 + half]
-        source = [block[a : a + 1, :] for a in range(3)]
+    def near_eval(place, half, wave, sign, own=False):
+        slot = 4 + half if own else near_place(place) * 2 + half
+        source = [pos_all[slot, a] for a in range(3)]
         for chunk in range(HALF // CHUNK):
             rows = slice(chunk * CHUNK, (chunk + 1) * CHUNK)
             target = [target_ref[a, rows, :] for a in range(3)]
@@ -302,12 +306,12 @@
                     start = part * UNKNOWNS + a * HALF + chunk * CHUNK
                     far_k[number * 2 + half, start : start + CHUNK, :] = value.astype(jnp.bfloat16)
 
-    def eval_near_from(start, stop, wave, sign):
+    def eval_near_others(wave, sign):
         def go(index, carry):
-            near_eval(lax.div(index, 2), lax.rem(index, 2), wave, sign, start == 0)
+            near_eval(lax.div(index, 2), lax.rem(index, 2), wave, sign)
             return carry
 
-        lax.fori_loop(2 * start, 2 * stop, go, 0)
+        lax.fori_loop(2, 6, go, 0)
 
     def eval_far(start, stop, wave, sign):
         def go(index, carry):
@@ -315,6 +319,10 @@
             return carry
 
         lax.fori_loop(2 * start, 2 * stop, go, 0)
+
+    def multiply_own(phase):
+        near_wait(*raw_set[phase], 5 - my_half)
+        acc_ref[...] = dot_nt(raw_all[phase][4], near_k[0]) + dot_nt(raw_all[phase][5], near_k[1])
 
     def multiply_near(phase):
         def go(place, carry):
@@ -324,7 +332,7 @@
             )
             return carry
 
-        lax.fori_loop(0, 3, go, 0)
+        lax.fori_loop(1, 3, go, 0)
 
     def multiply_far(phase):
         def go(number, carry):
@@ -357,18 +365,19 @@
     ]
     for load in loads:
         load.start()
-    acc_ref[...] = jnp.zeros_like(acc_ref)
     loads[0].wait()
     for a in range(3):
-        target_ref[a] = jnp.broadcast_to(pos_all[own_slot, a : a + 1, :], (HALF, HALF)).T
+        target_ref[a] = jnp.broadcast_to(pos_all[own_slot, a], (HALF, HALF)).T
+    near_eval(0, my_half, fund_wave, 1.0, True)
     loads[1].wait()
     loads[2].wait()
+    loads[3].wait()
+    pl.semaphore_wait(barrier, tiles)
+    partner_send(*pos_set)
+    near_sends(*pos_set)
+    near_sends(*raw_set[0])
     partial(0, raw_all[0][own_slot], vf_ref)
-    pl.semaphore_wait(barrier, tiles)
-    near_sends(*pos_set)
-    part_copy(0).start()
-    near_sends(*raw_set[0])
-    loads[3].wait()
+    partner_send(*raw_set[0])
 
     near_wait(*pos_set, 5 - my_half)
     skeleton = skel_ref[...]
@@ -376,11 +385,10 @@
     point = skeleton - component * POINTS
     lines = lax.broadcasted_iota(jnp.int32, (HALF, HALF), 0)
     masks = [lines + HALF * h == point for h in range(2)]
-    other = pos_all[4 + (1 - my_half)]
     packet = []
     for a in range(3):
         own_column = target_ref[a]
-        other_column = jnp.broadcast_to(other[a : a + 1, :], (HALF, HALF)).T
+        other_column = jnp.broadcast_to(pos_all[5 - my_half, a], (HALF, HALF)).T
         columns = [
             jnp.where(my_half == 0, own_column, other_column),
             jnp.where(my_half == 0, other_column, own_column),
@@ -395,17 +403,18 @@
     send_charges(0)
 
     near_forward(*pos_set)
-    eval_near_from(0, 1, fund_wave, 1.0)
+    near_eval(0, 1 - my_half, fund_wave, 1.0, True)
+    multiply_own(0)
     far_forward(*skel_set)
-    near_arrive(*pos_set, False)
-    eval_near_from(1, 3, fund_wave, 1.0)
+    near_arrive(*pos_set)
+    eval_near_others(fund_wave, 1.0)
     near_forward(*raw_set[0])
     far_arrive(*skel_set)
     split = (tiles - 3) // 2
     eval_far(0, split, fund_wave, 1.0)
     far_forward(*chg_set[0])
     eval_far(split, tiles - 3, fund_wave, 1.0)
-    near_arrive(*raw_set[0], True)
+    near_arrive(*raw_set[0])
     multiply_near(0)
     far_arrive(*chg_set[0])
     multiply_far(0)
@@ -424,18 +433,19 @@
     ).astype(jnp.bfloat16)
 
     raw_all[1][own_slot] = source
+    near_sends(*raw_set[1])
     partial(1, source, vh_ref)
-    part_copy(1).start()
-    near_sends(*raw_set[1])
-    acc_ref[...] = jnp.zeros_like(acc_ref)
-    eval_near_from(0, 1, harm_wave, -1.0)
+    partner_send(*raw_set[1])
+    near_eval(0, my_half, harm_wave, -1.0, True)
     send_charges(1)
-    eval_near_from(1, 3, harm_wave, -1.0)
+    near_eval(0, 1 - my_half, harm_wave, -1.0, True)
+    multiply_own(1)
+    eval_near_others(harm_wave, -1.0)
     near_forward(*raw_set[1])
     eval_far(0, split, harm_wave, -1.0)
     far_forward(*chg_set[1])
     eval_far(split, tiles - 3, harm_wave, -1.0)
-    near_arrive(*raw_set[1], True)
+    near_arrive(*raw_set[1])
     multiply_near(1)
     far_arrive(*chg_set[1])
     multiply_far(1)
@@ -474,7 +484,7 @@
                 pltpu.VMEM((SKELETONS, UNKNOWNS), bf16),
                 pltpu.VMEM((SKELETONS, UNKNOWNS), bf16),
                 pltpu.VMEM((3, HALF, HALF), f32),
-                pltpu.VMEM((10, 3, HALF), f32),
+                pltpu.VMEM((10, 3, 1, HALF), f32),
                 pltpu.VMEM((slabs, 8, HALF), f32),
                 pltpu.VMEM((10, ROWS, UNKNOWNS), bf16),
                 pltpu.VMEM((10, ROWS, UNKNOWNS), bf16),
@@ -498,13 +508,13 @@
                 dma((7,)),
             ],
             compiler_params=pltpu.CompilerParams(
-                collective_id=0, has_side_effects=True, vmem_limit_bytes=50 * 2**20
+                collective_id=0, has_side_effects=True, vmem_limit_bytes=VMEM
             ),
             name="images",
         )(
             fields,
             incident.reshape(ROWS, UNKNOWNS),
-            positions[0],
+            jnp.transpose(positions, (1, 0, 2)),
             chi,
             skeletons,
             near,

time: 41.2 us -> 36.9 us (0.90)
  local copies, waits for them, and re-layouts: 6.09 us -> 2.22 us
    unnamed x19 -> x4, local copies, waits for them, and re-layouts: 6.09 us -> 2.22 us
where the time goes in v2:
time: 36.9 us; the launch traced here: 36.7 us
  Pallas kernels  33.8 us (92%)
  local copies, waits for them, and re-layouts  2.22 us (6%)
  between operations  0.65 us (2%)
    pallas_call x1, Pallas kernels, on_device(): pl.pallas_call(lambda *refs: body(slabs, *refs), out_shape=(out, out), in...  33.8 us
    unnamed x4, local copies, waits for them, and re-layouts  2.22 us

profile of v2, /device:TPU:0, one launch (start us, length us, event | category | flops | bytes accessed | tf_op | source)
XLA Modules:
  0.0 36.7 jit_solution(14473820549065372845)
XLA Ops:
  0.6 33.8 %images.1 = (f32[64,384]{1,0:T(8,128)}, f32[64,384]{1,0:T(8,128)}) custom-call(bf16[64,384]{1,0:T(8,128)(2,1)} %bitcast.11, bf16[64,384]{1,0:T(8,128)(2,1)} %bitcast.12, f32[3,1,128]{2,1,0:T(1,128)} %bitcast.13, f32[1,128]{1,0:T(1,128)} %refs_3_.1, s32[1,128]{1,0:T(1,128)} %refs_4_.1, s32[1,2]{1,0:T(1,128)} %refs_5_.1, bf16[256,384]{1,0:T(8,128)(2,1)} %bitcast.7, ...), custom_call_target="tpu_custom_call" | custom-call | tf_op jit(solution)/shard_map/images/pallas_call | solution.py:475
  34.5 0.0 copy-start
  34.5 1.6 %copy.12 = f32[1,2,32,384]{3,2,1,0:T(8,128)} copy(f32[1,2,32,384]{3,2,1,0:T(8,128)} %bitcast.10) | data formatting | bytes 196608
  36.1 0.0 copy-done
  36.1 0.6 %copy.13 = f32[1,2,32,384]{3,2,1,0:T(8,128)} copy(f32[1,2,32,384]{3,2,1,0:T(8,128)S(1)} %bitcast.9) | data formatting | bytes 196608
Async XLA Ops:
  34.5 1.6 %copy-start = (f32[64,384]{1,0:T(8,128)S(1)}, f32[64,384]{1,0:T(8,128)}, u32[]{:S(2)}) copy-start(f32[64,384]{1,0:T(8,128)} %get-tuple-element.5) | copy-start | bytes 294916

commit v3 on v2

--- a/solution.py
+++ b/solution.py
@@ -410,12 +410,10 @@
     eval_near_others(fund_wave, 1.0)
     near_forward(*raw_set[0])
     far_arrive(*skel_set)
-    split = (tiles - 3) // 2
-    eval_far(0, split, fund_wave, 1.0)
-    far_forward(*chg_set[0])
-    eval_far(split, tiles - 3, fund_wave, 1.0)
+    eval_far(0, tiles - 3, fund_wave, 1.0)
     near_arrive(*raw_set[0])
     multiply_near(0)
+    far_forward(*chg_set[0])
     far_arrive(*chg_set[0])
     multiply_far(0)
 
@@ -442,11 +440,10 @@
     multiply_own(1)
     eval_near_others(harm_wave, -1.0)
     near_forward(*raw_set[1])
-    eval_far(0, split, harm_wave, -1.0)
-    far_forward(*chg_set[1])
-    eval_far(split, tiles - 3, harm_wave, -1.0)
+    eval_far(0, tiles - 3, harm_wave, -1.0)
     near_arrive(*raw_set[1])
     multiply_near(1)
+    far_forward(*chg_set[1])
     far_arrive(*chg_set[1])
     multiply_far(1)
     real, imag = combined()

time: 36.9 us -> 38.1 us (1.033); the launches traced: 36.7 us -> 37.5 us
  Pallas kernels: 33.8 us -> 34.6 us
    pallas_call x1, Pallas kernels: 33.8 us -> 34.6 us  [on_device(): pl.pallas_call(lambda *refs: body(slabs, *refs), out_shape=(out, out), in...]
where the time goes in v3:
time: 38.1 us; the launch traced here: 37.5 us
  Pallas kernels  34.6 us (91%)
  local copies, waits for them, and re-layouts  2.22 us (6%)
  between operations  0.65 us (2%)
    pallas_call x1, Pallas kernels, on_device(): pl.pallas_call(lambda *refs: body(slabs, *refs), out_shape=(out, out), in...  34.6 us
    unnamed x4, local copies, waits for them, and re-layouts  2.22 us

profile of v3, /device:TPU:0, one launch (start us, length us, event | category | flops | bytes accessed | tf_op | source)
XLA Modules:
  0.0 37.5 jit_solution(1830609379933054156)
XLA Ops:
  0.6 34.6 %images.1 = (f32[64,384]{1,0:T(8,128)}, f32[64,384]{1,0:T(8,128)}) custom-call(bf16[64,384]{1,0:T(8,128)(2,1)} %bitcast.11, bf16[64,384]{1,0:T(8,128)(2,1)} %bitcast.12, f32[3,1,128]{2,1,0:T(1,128)} %bitcast.13, f32[1,128]{1,0:T(1,128)} %refs_3_.1, s32[1,128]{1,0:T(1,128)} %refs_4_.1, s32[1,2]{1,0:T(1,128)} %refs_5_.1, bf16[256,384]{1,0:T(8,128)(2,1)} %bitcast.7, ...), custom_call_target="tpu_custom_call" | custom-call | tf_op jit(solution)/shard_map/images/pallas_call | solution.py:472
  35.2 0.0 copy-start
  35.3 1.6 %copy.12 = f32[1,2,32,384]{3,2,1,0:T(8,128)} copy(f32[1,2,32,384]{3,2,1,0:T(8,128)} %bitcast.10) | data formatting | bytes 196608
  36.8 0.0 copy-done
  36.8 0.6 %copy.13 = f32[1,2,32,384]{3,2,1,0:T(8,128)} copy(f32[1,2,32,384]{3,2,1,0:T(8,128)S(1)} %bitcast.9) | data formatting | bytes 196608
Async XLA Ops:
  35.2 1.6 %copy-start = (f32[64,384]{1,0:T(8,128)S(1)}, f32[64,384]{1,0:T(8,128)}, u32[]{:S(2)}) copy-start(f32[64,384]{1,0:T(8,128)} %get-tuple-element.5) | copy-start | bytes 294916

commit v4 on v2

--- a/solution.py
+++ b/solution.py
@@ -286,9 +286,8 @@
                         value = value.astype(jnp.bfloat16)
                         for p, q in [(a, b), (b, a)][: 1 + (a != b)]:
                             start = part * UNKNOWNS + p * HALF + chunk * CHUNK
-                            near_k[
-                                place * 2 + half, start : start + CHUNK, q * HALF : (q + 1) * HALF
-                            ] = value
+                            first_lane = pl.multiple_of(half * UNKNOWNS + q * HALF, HALF)
+                            near_k[place, start : start + CHUNK, pl.ds(first_lane, HALF)] = value
 
     def far_eval(number, half, wave, sign):
         block = skel_all[far_tile(number) * 2 + half]
@@ -322,14 +321,14 @@
 
     def multiply_own(phase):
         near_wait(*raw_set[phase], 5 - my_half)
-        acc_ref[...] = dot_nt(raw_all[phase][4], near_k[0]) + dot_nt(raw_all[phase][5], near_k[1])
+        fields = jnp.concatenate([raw_all[phase][4], raw_all[phase][5]], axis=1)
+        acc_ref[...] = dot_nt(fields, near_k[0])
 
     def multiply_near(phase):
         def go(place, carry):
             slot = near_place(place) * 2
-            acc_ref[...] += dot_nt(raw_all[phase][slot], near_k[place * 2]) + dot_nt(
-                raw_all[phase][slot + 1], near_k[place * 2 + 1]
-            )
+            fields = jnp.concatenate([raw_all[phase][slot], raw_all[phase][slot + 1]], axis=1)
+            acc_ref[...] += dot_nt(fields, near_k[place])
             return carry
 
         lax.fori_loop(1, 3, go, 0)
@@ -492,7 +491,7 @@
                 pltpu.VMEM((slabs, ROWS, HALF), bf16),
                 pltpu.VMEM((2, 2, ROWS, HALF), f32),
                 pltpu.VMEM((2, ROWS, HALF), f32),
-                pltpu.VMEM((6, 2 * UNKNOWNS, UNKNOWNS), bf16),
+                pltpu.VMEM((3, 2 * UNKNOWNS, 2 * UNKNOWNS), bf16),
                 pltpu.VMEM((2 * (tiles - 3), 2 * UNKNOWNS, HALF), bf16),
                 pltpu.VMEM((ROWS, 2 * UNKNOWNS), f32),
                 dma((9,)),

time: 36.9 us -> 37.1 us (level)
  no operation moved by 1% of the time
where the time goes in v4:
time: 37.1 us; the launch traced here: 36.9 us
  Pallas kernels  34 us (92%)
  local copies, waits for them, and re-layouts  2.22 us (6%)
  between operations  0.65 us (2%)
    pallas_call x1, Pallas kernels, on_device(): pl.pallas_call(lambda *refs: body(slabs, *refs), out_shape=(out, out), in...  34 us
    unnamed x4, local copies, waits for them, and re-layouts  2.22 us

profile of v4, /device:TPU:0, one launch (start us, length us, event | category | flops | bytes accessed | tf_op | source)
XLA Modules:
  0.0 36.9 jit_solution(2426384251569254796)
XLA Ops:
  0.6 34.0 %images.1 = (f32[64,384]{1,0:T(8,128)}, f32[64,384]{1,0:T(8,128)}) custom-call(bf16[64,384]{1,0:T(8,128)(2,1)} %bitcast.11, bf16[64,384]{1,0:T(8,128)(2,1)} %bitcast.12, f32[3,1,128]{2,1,0:T(1,128)} %bitcast.13, f32[1,128]{1,0:T(1,128)} %refs_3_.1, s32[1,128]{1,0:T(1,128)} %refs_4_.1, s32[1,2]{1,0:T(1,128)} %refs_5_.1, bf16[256,384]{1,0:T(8,128)(2,1)} %bitcast.7, ...), custom_call_target="tpu_custom_call" | custom-call | tf_op jit(solution)/shard_map/images/pallas_call | solution.py:474
  34.7 0.0 copy-start
  34.7 1.6 %copy.12 = f32[1,2,32,384]{3,2,1,0:T(8,128)} copy(f32[1,2,32,384]{3,2,1,0:T(8,128)} %bitcast.10) | data formatting | bytes 196608
  36.3 0.0 copy-done
  36.3 0.6 %copy.13 = f32[1,2,32,384]{3,2,1,0:T(8,128)} copy(f32[1,2,32,384]{3,2,1,0:T(8,128)S(1)} %bitcast.9) | data formatting | bytes 196608
Async XLA Ops:
  34.7 1.6 %copy-start = (f32[64,384]{1,0:T(8,128)S(1)}, f32[64,384]{1,0:T(8,128)}, u32[]{:S(2)}) copy-start(f32[64,384]{1,0:T(8,128)} %get-tuple-element.5) | copy-start | bytes 294916
